TPU v7x, 512 devices: a whole 4x4x16 slice. The times are simulated.
512 devices in a mesh: section: 64 (over x, y, z_hi, core), tp: 8 (over z_lo).
Axes of the slice: x: 4, y: 4, z: 16 (z_hi: 2, z_lo: 8; z = z_hi * 8 + z_lo), core: 2. Of those that a mesh axis runs over, the one named last changes fastest.
Arguments:
- queries: bfloat16 [64, 128, 8192], P('section', None, 'tp')
- fresh_kv: bfloat16 [64, 128, 2048], P('section', 'tp'), may hold values from -6 to 6
- pool_kv: bfloat16 [64, 32, 64, 2048], P('section', None, None, 'tp'), may hold values from -6 to 6
- hit_pages: int32 [64, 64], P('section'), may hold values from 0 to 31
- hit_owners: int32 [64, 64, 1], P('section'), may hold values from 0 to 63; in each aligned block of 64 rows (0 to 63, 64 to 127, ..., all dimensions but the last counted through in order) at most 2 rows name the same one
- offsets: int32 [64], P('section'), may hold values from 64 to 4096
Outputs:
- attended: bfloat16 [64, 128, 8192], P('section', None, 'tp')
Inputs may be any that keep to these rules, and one draw needn't show every extreme that they name: `hit_owners`: within the list of one layer no owner appears more than 2 times, and some owner appears exactly 2 times.
All inputs are finite; a program needn't handle non-finite values.
Results may differ from a plain program's by a relative error of at most 0.003.
Values may be sent and summed in bfloat16 or wider, within the bound.
A program may use at most 64 MiB of HBM per device.

v0:
```python
import jax
import jax.numpy as jnp
from jax import lax
from jax.sharding import PartitionSpec as P

HEAD = 128
MOST = 2


def head_attention(query_rows, key_rows, values, visible):
    scores = jnp.dot(query_rows, key_rows.T, preferred_element_type=jnp.float32) * HEAD ** (-0.5)
    scores = jnp.where(visible, scores, jnp.float32(-1e30))
    row_max = jnp.max(scores, axis=1, keepdims=True)
    weights = jnp.where(visible, jnp.exp(scores - row_max), jnp.float32(0.0))
    row_sum = jnp.sum(weights, axis=1, keepdims=True)
    blended = (
        jnp.dot(weights.astype(jnp.bfloat16), values, preferred_element_type=jnp.float32) / row_sum
    )
    return blended.astype(jnp.bfloat16)


def local(queries, fresh_kv, pool_kv, hit_pages, hit_owners, offsets):
    owner_count = lax.axis_size("section")
    own_pool = pool_kv[0]
    page_ids = hit_pages[0]
    owners_of = hit_owners[0, :, 0]
    start_pos = offsets[0]
    hit_count = page_ids.shape[0]
    earlier = jnp.arange(hit_count)[None, :] < jnp.arange(hit_count)[:, None]
    same_owner = owners_of[:, None] == owners_of[None, :]
    rank_in = jnp.sum(jnp.logical_and(same_owner, earlier), axis=1)
    slot_of = owners_of * MOST + rank_in
    fresh_rows = lax.all_to_all(fresh_kv, "tp", split_axis=2, concat_axis=1, tiled=True)[0]
    matches = slot_of[:, None] == jnp.arange(owner_count * MOST)[None, :]
    request = jnp.sum(jnp.where(matches, page_ids[:, None], 0), axis=0)
    request = request.reshape(owner_count, MOST)
    picked = own_pool[lax.all_to_all(request, "section", split_axis=0, concat_axis=0, tiled=True)]
    received = lax.all_to_all(picked, "section", split_axis=0, concat_axis=0, tiled=True)
    page_len = own_pool.shape[1]
    width = own_pool.shape[2]
    flattened = received.reshape(owner_count * MOST, page_len, width)
    fetched = flattened[slot_of].reshape(hit_count * page_len, width)
    stacked = jnp.concatenate([fetched, fresh_rows], axis=0)
    span_len = fresh_rows.shape[0]
    prefix = jnp.arange(hit_count * page_len) < start_pos
    prefix = jnp.broadcast_to(prefix[None, :], (span_len, hit_count * page_len))
    causal = jnp.arange(span_len)[None, :] <= jnp.arange(span_len)[:, None]
    visible = jnp.concatenate([prefix, causal], axis=1)
    query_block = queries[0]
    head_count = query_block.shape[1] // HEAD
    per_head = query_block.reshape(span_len, head_count, HEAD).transpose(1, 0, 2)
    key_rows = stacked[:, :HEAD]
    values = stacked[:, HEAD:]

    def one_head(query_rows):
        return head_attention(query_rows, key_rows, values, visible)

    blended = lax.map(one_head, per_head)
    return blended.transpose(1, 0, 2).reshape(1, span_len, head_count * HEAD)


def solution(mesh):
    return jax.shard_map(
        local,
        mesh=mesh,
        in_specs=(
            P("section", None, "tp"),
            P("section", "tp", None),
            P("section", None, None, "tp"),
            P("section", None),
            P("section", None, None),
            P("section"),
        ),
        out_specs=P("section", None, "tp"),
        check_vma=False,
    )
```

profile of v0, /device:TPU:33, one launch (start us, length us, event | category | flops | bytes accessed | tf_op | source)
XLA Modules:
  0.0 301.6 jit_solution(2297463901736652131)
XLA Ops:
  0.0 0.9 convert_reduce_fusion
  1.6 0.7 select_reduce_fusion
  2.4 0.7 all_to_all.22
  3.1 20.5 %all-to-all-start = ((s32[64,1,2]{2,1,0:T(1,128)}), s32[64,1,2]{2,1,0:T(1,128)S(1)}, u32[]{:S(2)}, u32[]{:S(2)}) async-start(s32[64,1,2]{2,1,0:T(1,128)} %bitcast.7), calls=%async_computation | async-start | bytes 65536 | tf_op jit(solution)/shard_map/all_to_all | solution.py:37
  23.6 2.0 copy.46
  26.1 11.5 %reduce = bf16[2048,16]{1,0:T(8,128)(2,1)S(1)} reduce(bf16[2048,1,16]{2,1,0:T(2,128)(2,1)S(1)} %bitcast.60, bf16[]{:T(256)} %broadcast.60), dimensions={1}, to_apply=%bitcast.41.reduce_sub_computation | reduce | bytes 131074
  37.7 1.2 reshape.105
  38.8 1.3 all-to-all-done
  40.1 5.5 %all-to-all-start.2 = ((bf16[8,2,2048]{2,1,0:T(2,128)(2,1)}), bf16[8,2,2048]{2,1,0:T(2,128)(2,1)S(1)}, u32[]{:S(2)}, u32[]{:S(2)}) async-start(bf16[8,2,2048]{2,1,0:T(2,128)(2,1)} %reshape.105), calls=%async_computation.2 | async-start | bytes 131072 | tf_op jit(solution)/shard_map/all_to_all | solution.py:33
  45.9 2.8 gather_fusion
  48.7 5.3 %all-to-all-done.2 = bf16[8,2,2048]{2,1,0:T(2,128)(2,1)S(1)} async-done(((bf16[8,2,2048]{2,1,0:T(2,128)(2,1)}), bf16[8,2,2048]{2,1,0:T(2,128)(2,1)S(1)}, u32[]{:S(2)}, u32[]{:S(2)}) %all-to-all-start.2) | async-done | bytes 65568 | tf_op jit(solution)/shard_map/all_to_all | solution.py:33
  54.0 18.0 %all-to-all-start.1 = ((bf16[64,2,64,256]{3,2,1,0:T(8,128)(2,1)}), bf16[64,2,64,256]{3,2,1,0:T(8,128)(2,1)}, u32[]{:S(2)}, u32[]{:S(2)}) async-start(bf16[64,2,64,256]{3,2,1,0:T(8,128)(2,1)} %bitcast.58), calls=%async_computation.1 | async-start | bytes 8388608 | tf_op jit(solution)/shard_map/all_to_all | solution.py:38
  73.1 0.9 reshape.106
  74.6 192.9 %all-to-all-done.1 = bf16[64,2,64,256]{3,2,1,0:T(8,128)(2,1)} async-done(((bf16[64,2,64,256]{3,2,1,0:T(8,128)(2,1)}), bf16[64,2,64,256]{3,2,1,0:T(8,128)(2,1)}, u32[]{:S(2)}, u32[]{:S(2)}) %all-to-all-start.1) | async-done | bytes 4194336 | tf_op jit(solution)/shard_map/all_to_all | solution.py:38
  267.5 4.2 %gather_fusion.1 = bf16[64,64,256]{2,1,0:T(8,128)(2,1)} fusion(bf16[128,64,256]{2,1,0:T(8,128)(2,1)} %bitcast.10, s32[1024]{0:T(1024)S(1)} %pad_clamp_fusion), kind=kCustom, calls=%fused_computation.1 | custom fusion | bytes 4194560 | tf_op jit(solution)/shard_map/gather | solution.py:42
  271.7 2.7 pad_maximum_fusion
  274.4 26.2 %while.10 = (s32[]{:T(128)}, bf16[8,128,128]{2,1,0:T(8,128)(2,1)S(1)}, bf16[8,128,128]{1,2,0:T(8,128)(2,1)S(1)}, bf16[4224,128]{1,0:T(8,128)(2,1)}, pred[128,422...) while((s32[]{:T(128)}, bf16[8,128,128]{2,1,0:T(8,128)(2,1)S(1)}, ...), condition=%wide.region_5.6_spmd, body=%wide.region_2.5_spmd.sunk | while | flops 281722624 | bytes 10340949 | solution.py:58
  274.4 1.9 fusion.28
  277.6 1.9 fusion.28
  280.2 0.7 fusion.30
  280.9 1.9 fusion.28
  284.2 1.9 fusion.28
  286.8 0.7 fusion.30
  287.5 1.9 fusion.28
  290.0 0.7 fusion.30
  290.8 1.9 fusion.28
  293.3 0.7 fusion.30
  294.0 1.9 fusion.28
  296.6 0.7 fusion.30
  297.3 1.9 fusion.28
  299.9 0.7 fusion.30
  300.8 0.8 reshape.86
  (36 shorter events, 9.3 us)
Async XLA Ops:
  0.0 45.9 %copy-start = (bf16[1,32,64,256]{3,2,1,0:T(8,128)(2,1)S(1)}, bf16[1,32,64,256]{3,2,1,0:T(8,128)(2,1)}, u32[]{:S(2)}) copy-start(bf16[1,32,64,256]{3,2,1,0:T(8,128)(2,1)} %param.10) | copy-start | bytes 3145732
  3.1 37.0 %all-to-all-start = ((s32[64,1,2]{2,1,0:T(1,128)}), s32[64,1,2]{2,1,0:T(1,128)S(1)}, u32[]{:S(2)}, u32[]{:S(2)}) async-start(s32[64,1,2]{2,1,0:T(1,128)} %bitcast.7), calls=%async_computation | async-start | bytes 65536 | tf_op jit(solution)/shard_map/all_to_all | solution.py:37
  40.1 13.9 %all-to-all-start.2 = ((bf16[8,2,2048]{2,1,0:T(2,128)(2,1)}), bf16[8,2,2048]{2,1,0:T(2,128)(2,1)S(1)}, u32[]{:S(2)}, u32[]{:S(2)}) async-start(bf16[8,2,2048]{2,1,0:T(2,128)(2,1)} %reshape.105), calls=%async_computation.2 | async-start | bytes 131072 | tf_op jit(solution)/shard_map/all_to_all | solution.py:33
  54.0 18.7 %copy-start.1 = (bf16[1,128,1024]{2,1,0:T(8,128)(2,1)S(1)}, bf16[1,128,1024]{2,1,0:T(8,128)(2,1)}, u32[]{:S(2)}) copy-start(bf16[1,128,1024]{2,1,0:T(8,128)(2,1)} %param.8) | copy-start | bytes 786436
  54.0 18.9 %copy-start.2 = (s32[1,64,1]{1,2,0:T(1,128)S(1)}, s32[1,64,1]{1,2,0:T(1,128)}, u32[]{:S(2)}) copy-start(s32[1,64,1]{1,2,0:T(1,128)} %param.12) | copy-start | bytes 772
  54.0 213.6 %all-to-all-start.1 = ((bf16[64,2,64,256]{3,2,1,0:T(8,128)(2,1)}), bf16[64,2,64,256]{3,2,1,0:T(8,128)(2,1)}, u32[]{:S(2)}, u32[]{:S(2)}) async-start(bf16[64,2,64,256]{3,2,1,0:T(8,128)(2,1)} %bitcast.58), calls=%async_computation.1 | async-start | bytes 8388608 | tf_op jit(solution)/shard_map/all_to_all | solution.py:38
where the time goes:
time: 302 us
  waiting for transfers between devices  199 us (66%)
  starting transfers between devices  44 us (15%)
  other arithmetic  22.1 us (7%)
  matrix products  20.6 us (7%)
  local copies, waits for them, and re-layouts  14.3 us (5%)
    all_to_all x1, waiting for transfers between devices, local(): lax.all_to_all(picked, 'section', split_axis=0, concat_axis=0, tiled=True)  193 us
    all_to_all x1, starting transfers between devices, local(): lax.all_to_all(request, 'section', split_axis=0, concat_axis=0, tiled=True)  20.5 us
    all_to_all x1, starting transfers between devices, local(): lax.all_to_all(picked, 'section', split_axis=0, concat_axis=0, tiled=True)  18 us
    dot_general x8, matrix products, head_attention(): jnp.dot(query_rows, key_rows.T, preferred_element_type=jnp.float32)  15.1 us
    unnamed x1, other arithmetic  11.5 us
  transfers between devices with their start and end apart: 3, of which 3 were waited for; matrix products, arithmetic and copies ran while one was open for 7% of the time, Pallas kernels for 0%

commit v1 on v0

v1 whole, which is shorter than its diff:
```python
import math

import jax
import jax.numpy as jnp
from jax import lax
from jax.experimental import pallas as pl
from jax.experimental.pallas import tpu as pltpu
from jax.sharding import PartitionSpec as P

HEAD = 128
HEADS = 8
PAGE = 64
MASKED = -1e30
TO_LOG2 = HEAD ** (-0.5) * math.log2(math.e)
FULL = 32767.0

MESH = pl.DeviceIdType.MESH
X_UP, X_DOWN = (1, 0, 0, 0), (3, 0, 0, 0)
Z_UP, Z_DOWN, Z_FAR = (0, 0, 1, 0), (0, 0, 15, 0), (0, 0, 8, 0)
Y_AWAY = [(0, d, 0, 0) for d in (1, 2, 3)]
CORE = (0, 0, 0, 1)


def place():
    section, z_lo = lax.axis_index("section"), lax.axis_index("tp")
    return section // 16, (section // 4) % 4, ((section // 2) % 2) * 8 + z_lo, section % 2


def device(delta):
    x, y, z, core = place()
    x, y, z, core = (x + delta[0]) % 4, (y + delta[1]) % 4, (z + delta[2]) % 16, (core + delta[3]) % 2
    return ((x * 4 + y) * 2 + z // 8) * 2 + core, z % 8


def remote(source, target, send, arrive, where):
    return pltpu.make_async_remote_copy(
        src_ref=source,
        dst_ref=target,
        send_sem=send,
        recv_sem=arrive,
        device_id=where,
        device_id_type=MESH,
    )


def column(row, size):
    down = lax.broadcasted_iota(jnp.int32, (size, size), 0)
    along = lax.broadcasted_iota(jnp.int32, (size, size), 1)
    return jnp.sum(jnp.where(down == along, row, 0), axis=1, keepdims=True)


def slot_table(pages, owners, offset):
    hits = pages.shape[1]
    down = lax.broadcasted_iota(jnp.int32, (hits, hits), 0)
    along = lax.broadcasted_iota(jnp.int32, (hits, hits), 1)
    owner_column = column(owners, hits)
    page_column = column(pages, hits)
    same = jnp.logical_and(owner_column == owners, along < down)
    rank = jnp.sum(jnp.where(same, 1, 0), axis=1, keepdims=True)
    slot = owner_column * 2 + rank
    match = slot == lax.broadcasted_iota(jnp.int32, (hits, 128), 1)
    first = lax.broadcasted_iota(jnp.int32, (hits, 128), 0) * PAGE
    rows = jnp.clip(offset - first, 0, PAGE)
    page_of = jnp.sum(jnp.where(match, page_column, 0), axis=0, keepdims=True)
    rows_of = jnp.sum(jnp.where(match, rows, 0), axis=0, keepdims=True)
    return page_of, rows_of


def coded(blend, low=1e-30):
    top = jnp.maximum(jnp.max(jnp.abs(blend), axis=0, keepdims=True), low)
    return jnp.round(blend * (FULL / top)).astype(jnp.int32).astype(jnp.int16), top * (1.0 / FULL)


def kernel(
    offset_ref, queries_ref, fresh_ref, pages_ref, owners_ref, pool_ref, out_ref,
    pool_00, pool_01, pool_10, pool_11, pool_20, pool_21, pool_30, pool_31, query_hops, query_all, table, table_s, fresh, keys, values_t, unit,
    part, part_stat, arrived, arrived_stat, back_hops, back_stat, back_stat_in,
    total, top_all, sum_all,
    local_sem, pool_send, pool_recv, core_send, core_recv, hop_send, hop_recv,
    spread_send, spread_recv, table_send, table_recv, fresh_send, fresh_recv,
    part_send, part_recv, stat_send, stat_recv, back_send, back_recv, home_send, home_recv,
):
    pools = ((pool_00, pool_01), (pool_10, pool_11), (pool_20, pool_21), (pool_30, pool_31))
    x, y, z, core = place()
    z_lo = lax.axis_index("tp")
    section = lax.axis_index("section")

    def tp_device(step):
        return section, (z_lo + step) % 8

    barrier = pltpu.get_barrier_semaphore()
    partners = [device(d) for d in [Z_FAR, Z_UP, Z_DOWN, X_UP, X_DOWN, CORE] + Y_AWAY]
    partners += [tp_device(step) for step in range(1, 8)]
    for partner in partners:
        pl.semaphore_signal(barrier, inc=1, device_id=partner, device_id_type=MESH)

    own_pool = pltpu.make_async_copy(pool_ref.at[0], pool_00, local_sem.at[0])
    own_pool.start()
    for h in range(HEADS):
        turned = queries_ref[0, :, h * HEAD:(h + 1) * HEAD].T
        query_hops[0, h] = turned
        query_all[0, 0, h] = turned
    page_of, rows_of = slot_table(pages_ref[...], owners_ref[...], offset_ref[0])
    table[0, 0, 0:1] = page_of
    table[0, 0, 1:2] = rows_of
    fresh[z_lo] = fresh_ref[0, :, pl.ds(pl.multiple_of(z_lo * 256, 256), 256)]
    first_row = lax.broadcasted_iota(jnp.int32, (128, 256), 0) == 0
    unit[...] = jnp.where(first_row, 1.0, 0.0).astype(jnp.bfloat16)
    own_pool.wait()

    pl.semaphore_wait(barrier, len(partners))

    def query_hop(step, h):
        return remote(
            query_hops.at[step, h], query_hops.at[step + 1, h],
            hop_send.at[step, h], hop_recv.at[step, h], device((Z_UP, Z_DOWN)[h % 2]),
        )

    def spread(group, h, away):
        source = query_hops.at[0 if group == 0 else 8, pl.ds(h, 2)]
        return remote(
            source, query_all.at[group, 4 - away, pl.ds(h, 2)],
            spread_send.at[group, away - 1, h // 2], spread_recv.at[group, away - 1, h // 2],
            device((0, away, 0, 0)),
        )

    def table_spread(group, away):
        return remote(
            table.at[group, 0], table.at[group, 4 - away],
            table_send.at[group, away - 1], table_recv.at[group, away - 1], device((0, away, 0, 0)),
        )

    for h in range(HEADS):
        query_hop(0, h).start()
    table_far = remote(table.at[0, 0], table.at[1, 0], table_send.at[2, 0], table_recv.at[2, 0], device(Z_FAR))
    table_far.start()
    low, high = pl.ds(0, 16), pl.ds(16, 16)
    mine = pool_00
    up_low = remote(mine.at[low], pool_10.at[low], pool_send.at[0], pool_recv.at[0], device(X_UP))
    down_high = remote(mine.at[high], pool_30.at[high], pool_send.at[1], pool_recv.at[1], device(X_DOWN))
    up_high = remote(mine.at[high], pool_10.at[high], pool_send.at[2], pool_recv.at[2], device(X_UP))
    down_low = remote(mine.at[low], pool_30.at[low], pool_send.at[3], pool_recv.at[3], device(X_DOWN))
    over_low = remote(pool_10.at[low], pool_20.at[low], pool_send.at[4], pool_recv.at[4], device(X_UP))
    over_high = remote(pool_30.at[high], pool_20.at[high], pool_send.at[5], pool_recv.at[5], device(X_DOWN))
    for copy in (up_low, down_high, up_high, down_low):
        copy.start()

    def across(chip):
        return remote(
            pools[chip][0], pools[chip][1], core_send.at[chip], core_recv.at[chip], device(CORE)
        )

    across(0).start()
    for away in (1, 2, 3):
        table_spread(0, away).start()
    fresh_copies = []
    for step in range(1, 8):
        columns = pl.ds(pl.multiple_of(((z_lo + step) % 8) * 256, 256), 256)
        copy = remote(
            fresh_ref.at[0, :, columns], fresh.at[z_lo],
            fresh_send.at[step - 1], fresh_recv.at[step - 1], tp_device(step),
        )
        copy.start()
        fresh_copies.append(copy)
    for h in range(0, HEADS, 2):
        for away in (1, 2, 3):
            spread(0, h, away).start()

    def query_step(step):
        for h in range(HEADS):
            query_hop(step - 1, h).wait_recv()
            query_hop(step, h).start()

    query_step(1)
    query_step(2)
    table_far.wait_recv()
    for away in (1, 2, 3):
        table_spread(1, away).start()
    query_step(3)

    for copy in fresh_copies:
        copy.wait_recv()
    fresh_all = fresh[...].reshape(128, 256)
    fresh_keys, fresh_values_t = fresh_all[:, :HEAD], fresh_all[:, HEAD:].T
    key_at = lax.broadcasted_iota(jnp.int32, (128, 128), 0)
    row_at = lax.broadcasted_iota(jnp.int32, (128, 128), 1)
    for h in range(HEADS):
        scores = jnp.dot(fresh_keys, query_all[0, 0, h], preferred_element_type=jnp.float32)
        scores = jnp.where(key_at <= row_at, scores, MASKED)
        top = jnp.max(scores, axis=0, keepdims=True)
        weights = jnp.exp2((scores - top) * TO_LOG2)
        total[h] = jnp.dot(fresh_values_t, weights.astype(jnp.bfloat16), preferred_element_type=jnp.float32)
        top_all[h] = top * TO_LOG2
        sum_all[h] = jnp.sum(weights, axis=0, keepdims=True)

    query_step(4)
    up_low.wait_recv()
    over_low.start()
    down_high.wait_recv()
    over_high.start()
    for step in (5, 6, 7):
        query_step(step)
    for h in range(HEADS):
        query_hop(7, h).wait_recv()
        query_all[1, 0, h] = query_hops[8, h]
        if h % 2:
            for away in (1, 2, 3):
                spread(1, h - 1, away).start()

    for group in (0, 1):
        for away in (1, 2, 3):
            table_spread(group, away).wait_recv()
    to_scalar = pltpu.make_async_copy(table, table_s, local_sem.at[1])
    to_scalar.start()
    to_scalar.wait()

    lane = lax.broadcasted_iota(jnp.int32, (128, 128), 1)
    sublane = lax.broadcasted_iota(jnp.int32, (128, 128), 0)

    def lay_out(chip, side):
        owner = ((((x - chip + 4) % 4) * 4 + y) * 2 + z // 8) * 2 + (core + side) % 2
        at = (chip * 2 + side) * 128

        def one(layer, carry):
            group, near = layer // 4, layer % 4
            page_0, page_1 = table_s[group, near, 0, owner * 2], table_s[group, near, 0, owner * 2 + 1]
            rows_0, rows_1 = table_s[group, near, 1, owner * 2], table_s[group, near, 1, owner * 2 + 1]
            both = jnp.concatenate([pools[chip][side][page_0], pools[chip][side][page_1]], axis=0)
            keys[layer, at:at + 128, :HEAD] = both[:, :HEAD]
            values_t[layer, :, at:at + 128] = both[:, HEAD:].T
            seen = jnp.where(sublane < PAGE, rows_0 - sublane, rows_1 + PAGE - sublane) > 0
            hidden = jnp.logical_and(lane == 0, jnp.logical_not(seen))
            keys[layer, at:at + 128, HEAD:] = jnp.where(hidden, MASKED, 0.0).astype(jnp.bfloat16)
            return carry

        lax.fori_loop(0, 8, one, 0)

    lay_out(0, 0)
    up_high.wait_recv()
    across(1).start()
    lay_out(1, 0)
    down_low.wait_recv()
    across(3).start()
    lay_out(3, 0)
    for chip in (0, 1, 3):
        across(chip).wait_recv()
        lay_out(chip, 1)
    over_low.wait_recv()
    over_high.wait_recv()
    across(2).start()
    lay_out(2, 0)
    across(2).wait_recv()
    lay_out(2, 1)

    def partial(group, near, pair):
        layer = group * 4 + near
        heads = jnp.concatenate([query_all[group, near, 2 * pair], query_all[group, near, 2 * pair + 1]], axis=1)
        right = jnp.concatenate([heads, unit[...]], axis=0)
        scores = jnp.dot(keys[layer], right, preferred_element_type=jnp.float32)
        top = jnp.max(scores, axis=0, keepdims=True)
        weights = jnp.exp2((scores - top) * TO_LOG2)
        row_sum = jnp.sum(weights, axis=0, keepdims=True)
        blend = jnp.dot(values_t[layer], weights.astype(jnp.bfloat16), preferred_element_type=jnp.float32)
        code, scale = coded(blend)
        scale = scale / row_sum
        level = top * TO_LOG2 + jnp.log2(row_sum)
        for i in (0, 1):
            cut = slice(i * 128, (i + 1) * 128)
            part[group, near, 2 * pair + i] = code[:, cut]
            part_stat[group, near, 2 * pair + i, 0:1] = level[:, cut]
            part_stat[group, near, 2 * pair + i, 1:2] = scale[:, cut]

    def send_part(group, near, pair):
        heads = pl.ds(2 * pair, 2)
        return remote(
            part.at[group, near, heads], arrived.at[group, 3 - near, heads],
            part_send.at[group, near - 1, pair], part_recv.at[group, near - 1, pair], device((0, near, 0, 0)),
        )

    def send_stat(group, near, pair):
        heads = pl.ds(2 * pair, 2)
        return remote(
            part_stat.at[group, near, heads], arrived_stat.at[group, 3 - near, heads],
            stat_send.at[group, near - 1, pair], stat_recv.at[group, near - 1, pair], device((0, near, 0, 0)),
        )

    def partials(group, pair):
        def one(near, carry):
            partial(group, near, pair)
            return carry

        lax.fori_loop(0, 4, one, 0)
        for near in (1, 2, 3):
            send_part(group, near, pair).start()
            send_stat(group, near, pair).start()

    def received(group, pair):
        for near in (1, 2, 3):
            send_part(group, near, pair).wait_recv()
            send_stat(group, near, pair).wait_recv()

    def merged(group, h):
        codes = [part[group, 0, h]] + [arrived[group, i, h] for i in range(3)]
        stats = [part_stat[group, 0, h]] + [arrived_stat[group, i, h] for i in range(3)]
        top = stats[0][0:1]
        for stat in stats[1:]:
            top = jnp.maximum(top, stat[0:1])
        shares = [jnp.exp2(stat[0:1] - top) for stat in stats]
        row_sum = shares[0] + shares[1] + shares[2] + shares[3]
        blend = None
        for code, stat, share in zip(codes, stats, shares):
            term = code.astype(jnp.int32).astype(jnp.float32) * (share * stat[1:2])
            blend = term if blend is None else blend + term
        return blend, top, row_sum

    def back_hop(step, h):
        return remote(
            back_hops.at[step, h], back_hops.at[step + 1, h],
            back_send.at[step, h], back_recv.at[step, h], device((Z_UP, Z_DOWN)[h % 2]),
        )

    def home(pair):
        heads = pl.ds(2 * pair, 2)
        return remote(
            back_stat.at[heads], back_stat_in.at[heads], home_send.at[pair], home_recv.at[pair], device(Z_FAR)
        )

    for h in range(0, HEADS, 2):
        for away in (1, 2, 3):
            spread(1, h, away).wait_recv()
            spread(0, h, away).wait_recv()
    lax.fori_loop(0, 4, lambda pair, carry: (partials(1, pair), carry)[1], 0)
    for pair in range(4):
        received(1, pair)
        for i in (0, 1):
            h = 2 * pair + i
            blend, top, row_sum = merged(1, h)
            code, scale = coded(blend)
            back_hops[0, h] = code
            back_stat[h, 0:1] = top + jnp.log2(row_sum)
            back_stat[h, 1:2] = scale / row_sum
            back_hop(0, h).start()
        home(pair).start()

    def back_step(step):
        for h in range(HEADS):
            back_hop(step - 1, h).wait_recv()
            back_hop(step, h).start()

    def include(h, blend, top, row_sum):
        new = jnp.maximum(top_all[h], top)
        old_share, share = jnp.exp2(top_all[h] - new), jnp.exp2(top - new)
        total[h] = total[h] * old_share + blend * share
        sum_all[h] = sum_all[h] * old_share + row_sum * share
        top_all[h] = new

    for pair in range(4):
        partials(0, pair)
        back_step(pair + 1)
    for pair in range(4):
        received(0, pair)
        for h in (2 * pair, 2 * pair + 1):
            blend, top, row_sum = merged(0, h)
            include(h, blend, top, row_sum)
        if pair < 3:
            back_step(pair + 5)
    for pair in range(4):
        home(pair).wait_recv()
        for h in (2 * pair, 2 * pair + 1):
            back_hop(7, h).wait_recv()
            stat = back_stat_in[h]
            blend = back_hops[8, h].astype(jnp.int32).astype(jnp.float32) * stat[1:2]
            include(h, blend, stat[0:1], jnp.ones_like(stat[0:1]))
            result = total[h] / sum_all[h]
            out_ref[0, :, h * HEAD:(h + 1) * HEAD] = result.T.astype(jnp.bfloat16)

    for step in range(8):
        for h in range(HEADS):
            query_hop(step, h).wait_send()
            back_hop(step, h).wait_send()
    for copy in [up_low, up_high, down_low, down_high, over_low, over_high, table_far] + fresh_copies:
        copy.wait_send()
    for chip in range(4):
        across(chip).wait_send()
    for pair in range(4):
        home(pair).wait_send()
    for group in (0, 1):
        for away in (1, 2, 3):
            table_spread(group, away).wait_send()
            for pair in range(4):
                spread(group, 2 * pair, away).wait_send()
                send_part(group, away, pair).wait_send()
                send_stat(group, away, pair).wait_send()


def local(queries, fresh_kv, pool_kv, hit_pages, hit_owners, offsets):
    bf16, i16, f32 = jnp.bfloat16, jnp.int16, jnp.float32
    vmem, dma = pltpu.VMEM, pltpu.SemaphoreType.DMA
    in_vmem = pl.BlockSpec(memory_space=pltpu.VMEM)
    scratch = [
        *[vmem((32, PAGE, 256), bf16) for _ in range(8)],
        vmem((9, HEADS, HEAD, 128), bf16),
        vmem((2, 4, HEADS, HEAD, 128), bf16),
        vmem((2, 4, 2, 128), jnp.int32),
        pltpu.SMEM((2, 4, 2, 128), jnp.int32),
        vmem((8, 16, 256), bf16),
        vmem((8, 1024, 256), bf16),
        vmem((8, HEAD, 1024), bf16),
        vmem((128, 256), bf16),
        vmem((2, 4, HEADS, HEAD, 128), i16),
        vmem((2, 4, HEADS, 2, 128), f32),
        vmem((2, 3, HEADS, HEAD, 128), i16),
        vmem((2, 3, HEADS, 2, 128), f32),
        vmem((9, HEADS, HEAD, 128), i16),
        vmem((HEADS, 2, 128), f32),
        vmem((HEADS, 2, 128), f32),
        vmem((HEADS, HEAD, 128), f32),
        vmem((HEADS, 1, 128), f32),
        vmem((HEADS, 1, 128), f32),
        dma((2,)),
        dma((6,)), dma((6,)),
        dma((4,)), dma((4,)),
        dma((8, HEADS)), dma((8, HEADS)),
        dma((2, 3, 4)), dma((2, 3, 4)),
        dma((3, 3)), dma((3, 3)),
        dma((7,)), dma((7,)),
        dma((2, 3, 4)), dma((2, 3, 4)),
        dma((2, 3, 4)), dma((2, 3, 4)),
        dma((8, HEADS)), dma((8, HEADS)),
        dma((4,)), dma((4,)),
    ]
    return pl.pallas_call(
        kernel,
        out_shape=jax.ShapeDtypeStruct(queries.shape, queries.dtype),
        in_specs=[
            pl.BlockSpec(memory_space=pltpu.SMEM), in_vmem, in_vmem, in_vmem, in_vmem,
            pl.BlockSpec(memory_space=pl.ANY),
        ],
        out_specs=in_vmem,
        scratch_shapes=scratch,
        name="spanned_attention",
        compiler_params=pltpu.CompilerParams(
            collective_id=0, has_side_effects=True, vmem_limit_bytes=56 << 20
        ),
    )(offsets, queries, fresh_kv, hit_pages, hit_owners.reshape(1, -1), pool_kv)


def solution(mesh):
    return jax.shard_map(
        local,
        mesh=mesh,
        in_specs=(
            P("section", None, "tp"),
            P("section", "tp", None),
            P("section", None, None, "tp"),
            P("section", None),
            P("section", None, None),
            P("section"),
        ),
        out_specs=P("section", None, "tp"),
        check_vma=False,
    )
```

time: 302 us -> 114 us (0.38)
  the two profiles are of different devices: /device:TPU:33 before, /device:TPU:6 now
where the time goes in v1:
time: 114 us
  Pallas kernels  111 us (97%)
  local copies, waits for them, and re-layouts  1.67 us (1%)
    pallas_call x1, Pallas kernels, local(): pl.pallas_call(kernel, out_shape=jax.ShapeDtypeStruct(queries.shape, quer...  111 us

profile of v1, /device:TPU:6, one launch (start us, length us, event | category | flops | bytes accessed | tf_op | source)
XLA Modules:
  0.0 113.8 jit_solution(1930575301656976195)
XLA Ops:
  0.7 111.4 %spanned_attention.1 = bf16[1,128,1024]{2,1,0:T(8,128)(2,1)} custom-call(s32[1]{0:T(128)S(6)} %copy.8.offset_ref, bf16[1,128,1024]{2,1,0:T(8,128)(2,1)} %queries_ref.1, bf16[1,16,2048]{2,1,0:T(8,128)(2,1)} %fresh_ref.1, s32[1,64]{1,0:T(1,128)} %pages_ref.1, s32[1,64]{1,0:T(1,128)} %bitcast.1, bf16[1,32,64,256]{3,2,1,0:T(8,128)(2,1)} %pool_ref.1), custom_call_target="tpu_custom_call" | custom-call | tf_op jit(solution)/shard_map/spanned_attention/pallas_call | solution.py:432
  112.1 1.7 %copy.9 = bf16[1,128,1024]{2,1,0:T(8,128)(2,1)} copy(bf16[1,128,1024]{2,1,0:T(8,128)(2,1)} %spanned_attention.1) | data formatting | bytes 524288
